TPU v7x, 32 devices: a whole 2x2x4 slice. The times are simulated.
32 devices in a mesh: graph: 16 (over z, y, x), rep: 2 (over core).
Axes of the slice: x: 2, y: 2, z: 4, core: 2. Of those that a mesh axis runs over, the one named last changes fastest.
Arguments:
- grad_out: bfloat16 [8192, 256], P(('graph', 'rep')), may hold values from -6 to 6
- pre_act: bfloat16 [8192, 256], P(('graph', 'rep')), may hold values from -6 to 6
- aggregated: bfloat16 [8192, 256], P(('graph', 'rep')), may hold values from -0.3125 to 0.3125
- weight: bfloat16 [256, 256], replicated, may hold values from -0.375 to 0.375
- adj_tiles: bfloat16 [16, 2, 16, 2, 128, 128], P('graph', 'rep'), may hold values from 0 to 0.039794922
- tile_row: int32 [16, 2, 16, 2], P('graph', 'rep'), may hold values from 0 to 1
- tile_col: int32 [16, 2, 16, 2], P('graph', 'rep'), may hold values from 0 to 3
- tile_count: int32 [16, 2, 16], P('graph', 'rep'), may hold values from 0 to 2, as said below
- node_perm: int32 [16, 512], P('graph'), may hold values from 0 to 511, each once within a row
Outputs:
- input_grad: bfloat16 [8192, 256], P(('graph', 'rep'))
- weight_grad: float32 [256, 256], replicated
- relu_grad: bfloat16 [8192, 256], P(('graph', 'rep'))
Inputs may be any that keep to these rules, and one draw needn't show every extreme that they name: tile_count[g, r, g] is 2 for every partition g and replica r. `node_perm`: each row is a permutation.
All inputs are finite; a program needn't handle non-finite values.
Results may differ from a plain program's by a relative error of at most 0.0049.
Values may be sent and summed in bfloat16 or wider, within the bound.
A program may use at most 128 MiB of HBM per device.

v0:
```python
import jax
import jax.numpy as jnp
from jax import lax
from jax.sharding import PartitionSpec as P


def tile_products(running, sources, row_count, local_tiles, local_row, local_col, local_count):
    piece_parts = sources.shape[0] // row_count
    tile_size = local_tiles.shape[-1]
    feature_width = sources.shape[1]
    blocks = sources.reshape(piece_parts, row_count // tile_size, tile_size, feature_width)
    part_index = jnp.arange(piece_parts, dtype=jnp.int32)
    for slot_index in range(local_tiles.shape[1]):
        chosen = blocks[part_index, local_row[:, slot_index]]
        product = jnp.einsum(
            "kab,kac->kbc", local_tiles[:, slot_index], chosen, preferred_element_type=jnp.float32
        )
        alive = (local_count > slot_index).astype(jnp.float32)
        running = running.at[local_col[:, slot_index]].add(product * alive[:, None, None])
    return running


def body(
    grad_out, pre_act, aggregated, weight, adj_tiles, tile_row, tile_col, tile_count, node_perm
):
    row_count = grad_out.shape[0]
    feature_width = weight.shape[0]
    relu_grad = jnp.where(pre_act > 0, grad_out, jnp.zeros_like(grad_out))
    partial_weight = lax.dot_general(
        aggregated, relu_grad, (((0,), (0,)), ((), ())), preferred_element_type=jnp.float32
    )
    local_tiles = adj_tiles[0, 0]
    local_row = tile_row[0, 0]
    local_col = tile_col[0, 0]
    local_count = tile_count[0, 0]
    local_perm = node_perm[0]
    tile_size = local_tiles.shape[-1]
    col_blocks = lax.axis_size("rep") * (row_count // tile_size)
    empty = jnp.zeros((col_blocks, tile_size, feature_width), jnp.float32)
    back_agg = lax.dot_general(
        relu_grad, weight, (((1,), (1,)), ((), ())), preferred_element_type=jnp.float32
    ).astype(jnp.bfloat16)
    running = tile_products(
        empty,
        lax.all_gather(back_agg, "graph", axis=0, tiled=True),
        row_count,
        local_tiles,
        local_row,
        local_col,
        local_count,
    )
    partial_grad = running.reshape(col_blocks * tile_size, feature_width)
    input_grad = lax.psum_scatter(
        jnp.take(partial_grad, local_perm, axis=0), "rep", scatter_dimension=0, tiled=True
    ).astype(jnp.bfloat16)
    weight_grad = lax.psum(partial_weight, ("graph", "rep"))
    return (input_grad, weight_grad, relu_grad)


def solution(mesh):
    placed = (
        P(("graph", "rep"), None),
        P(("graph", "rep"), None),
        P(("graph", "rep"), None),
        P(),
        P("graph", "rep", None, None, None, None),
        P("graph", "rep", None, None),
        P("graph", "rep", None, None),
        P("graph", "rep", None),
        P("graph", None),
    )
    return jax.shard_map(
        body,
        mesh=mesh,
        in_specs=placed,
        out_specs=(P(("graph", "rep"), None), P(), P(("graph", "rep"), None)),
        check_vma=False,
    )
```

profile of v0, /device:TPU:0, one launch (start us, length us, event | category | flops | bytes accessed | tf_op | source)
XLA Modules:
  0.0 160.9 jit_solution(16786216906860122379)
XLA Ops:
  8.0 0.0 copy-start
  8.0 0.0 all-gather.2.cloned.1.call-start
  8.1 1.1 compare_select_fusion
  9.1 0.0 copy-done
  9.2 0.0 copy-start.1
  9.2 0.9 convolution_convert_fusion
  10.0 0.0 all-gather.2.cloned.1.call-update
  10.1 0.0 all-reduce.2.cloned.1.call-start
  10.1 1.8 %convolution_bitcast_fusion = f32[256,256]{0,1:T(8,128)} fusion(bf16[256,256]{1,0:T(8,128)(2,1)S(1)} %compare_select_fusion, bf16[256,256]{1,0:T(8,128)(2,1)} %param.11), kind=kOutput, calls=%fused_computation.7 | convolution fusion | flops 33554432 | bytes 524288 | tf_op jit(solution)/shard_map/dot_general | solution.py:29
  12.0 0.0 all-reduce.2.cloned.1.call-update
  12.0 0.0 reduce-scatter.2.cloned.1.call-start
  12.0 0.7 compare_select_fusion.1
  12.7 0.7 compare_and_fusion
  13.4 0.8 fusion.10
  14.2 0.8 fusion.6
  14.9 0.7 fusion.1
  15.6 0.1 copy.25
  15.7 60.0 %all-gather.2.cloned.1.call-done = bf16[4096,256]{1,0:T(8,128)(2,1)} async-done(((bf16[256,256]{1,0:T(8,128)(2,1)}), bf16[4096,256]{1,0:T(8,128)(2,1)}) %all-gather.2.cloned.1.call-update) | async-done | bytes 2097168 | tf_op jit(solution)/shard_map/all_gather | solution.py:45
  75.7 3.2 %gather_fusion.1 = bf16[16,128,256]{2,1,0:T(8,128)(2,1)} fusion(bf16[16,2,128,256]{3,2,1,0:T(8,128)(2,1)} %bitcast.44, s32[16]{0:T(128)S(1)} %get-tuple-element.9), kind=kCustom, calls=%fused_computation.1 | custom fusion | bytes 2097280 | tf_op jit(solution)/shard_map/gather | solution.py:14
  78.9 2.2 %gather_fusion = bf16[16,128,256]{2,1,0:T(8,128)(2,1)S(1)} fusion(bf16[16,2,128,256]{3,2,1,0:T(8,128)(2,1)} %bitcast.45, s32[16]{0:T(128)S(1)} %get-tuple-element.10), kind=kCustom, calls=%fused_computation | custom fusion | bytes 2097280 | tf_op jit(solution)/shard_map/gather | solution.py:14
  81.1 1.8 %multiply_bitcast_fusion.1 = f32[16,128,256]{1,2,0:T(8,128)} fusion(bf16[16,128,256]{2,1,0:T(8,128)(2,1)S(1)} %gather_fusion, f32[16]{0:T(128)S(1)} %get-tuple-element.14, bf16[16,2,128,128]{3,2,0,1:T(8,128)(2,1)S(1)} %bitcast.42), kind=kOutput, calls=%fused_computation.6 | convolution fusion | flops 134742016 | bytes 3670528 | tf_op jit(solution)/shard_map/kab,kac->kbc/dot_general | solution.py:15
  83.0 1.9 %copy.18 = f32[16,128,256]{2,1,0:T(8,128)S(1)} copy(f32[16,128,256]{1,2,0:T(8,128)} %multiply_bitcast_fusion.1) | data formatting | bytes 4194304 | tf_op jit(solution)/shard_map/mul | solution.py:19
  84.9 3.1 %multiply_bitcast_fusion = f32[16,128,256]{1,2,0:T(8,128)} fusion(bf16[16,128,256]{2,1,0:T(8,128)(2,1)} %gather_fusion.1, f32[16]{0:T(128)S(1)} %get-tuple-element.13, bf16[16,2,128,128]{3,2,0,1:T(8,128)(2,1)S(1)} %bitcast.43), kind=kOutput, calls=%fused_computation.5 | convolution fusion | flops 134742016 | bytes 3670528 | tf_op jit(solution)/shard_map/kab,kac->kbc/dot_general | solution.py:15
  88.0 2.9 %copy.20 = f32[16,128,256]{2,1,0:T(8,128)} copy(f32[16,128,256]{1,2,0:T(8,128)} %multiply_bitcast_fusion) | data formatting | bytes 4194304 | tf_op jit(solution)/shard_map/mul | solution.py:19
  90.9 2.2 %scatter_fusion = f32[4,128,256]{2,1,0:T(8,128)S(1)} fusion(f32[4,128,256]{2,1,0:T(8,128)S(1)} %broadcast_in_dim.10, s32[16]{0:T(128)S(1)} %get-tuple-element.12, f32[16,128,256]{2,1,0:T(8,128)S(1)} %copy.18), kind=kCustom, calls=%fused_computation.3 | custom fusion | flops 524288 | bytes 6291520 | tf_op jit(solution)/shard_map/scatter-add | solution.py:19
  93.1 3.5 %scatter_fusion.1 = f32[4,128,256]{2,1,0:T(8,128)S(1)} fusion(f32[4,128,256]{2,1,0:T(8,128)S(1)} %scatter_fusion, s32[16]{0:T(128)S(1)} %get-tuple-element.11, f32[16,128,256]{2,1,0:T(8,128)} %copy.20), kind=kCustom, calls=%fused_computation.4 | custom fusion | flops 524288 | bytes 6291520 | tf_op jit(solution)/shard_map/scatter-add | solution.py:19
  96.6 1.6 gather_fusion.2
  98.2 0.9 broadcast_select_fusion
  99.1 0.0 reduce-scatter.2.cloned.1.call-update
  99.1 51.0 %all-reduce.2.cloned.1.call-done = f32[256,256]{0,1:T(8,128)} async-done(((f32[256,256]{0,1:T(8,128)}), f32[256,256]{0,1:T(8,128)}) %all-reduce.2.cloned.1.call-update) | async-done | bytes 262160 | tf_op jit(solution)/shard_map/psum | solution.py:56
  150.1 1.8 %copy.21 = f32[256,256]{1,0:T(8,128)} copy(f32[256,256]{0,1:T(8,128)} %all-reduce.2.cloned.1.call-done) | data formatting | bytes 524288
  151.9 1.6 %convert_element_type.31 = bf16[256,256]{1,0:T(8,128)(2,1)} convert(f32[256,256]{1,0:T(8,128)} %reduce-scatter.2.cloned.1.call-done) | non-fusion elementwise | flops 65536 | bytes 393216 | tf_op jit(solution)/shard_map/convert_element_type | solution.py:55
  (6 shorter events, 0.0 us)
Async XLA Ops:
  8.0 1.1 copy-start
  8.0 7.6 %copy-start.2 = (bf16[1,1,16,2,128,128]{5,4,3,2,1,0:T(8,128)(2,1)S(1)}, bf16[1,1,16,2,128,128]{5,4,3,2,1,0:T(8,128)(2,1)}, u32[]{:S(2)}) copy-start(bf16[1,1,16,2,128,128]{5,4,3,2,1,0:T(8,128)(2,1)} %param.13) | copy-start | bytes 3145732
  8.0 67.7 %all-gather.2.cloned.1.call-start = ((), (), s32[]{:S(2)}) async-start(), calls=%async_computation.1 | async-start | bytes 2228224 | tf_op jit(solution)/shard_map/all_gather | solution.py:45
  9.2 69.8 %copy-start.1 = (bf16[256,256]{1,0:T(8,128)(2,1)}, bf16[256,256]{1,0:T(8,128)(2,1)S(1)}, u32[]{:S(2)}) copy-start(bf16[256,256]{1,0:T(8,128)(2,1)S(1)} %compare_select_fusion) | copy-start | bytes 393220
  10.1 140.0 %all-reduce.2.cloned.1.call-start = ((), (), s32[]{:S(2)}) async-start(), calls=%async_computation.3 | async-start | bytes 524288 | tf_op jit(solution)/shard_map/psum | solution.py:56
  12.0 139.9 %reduce-scatter.2.cloned.1.call-start = ((), (), s32[]{:S(2)}) async-start(), calls=%async_computation.2 | async-start | bytes 786432 | tf_op jit(solution)/shard_map/reduce_scatter | solution.py:53
Sparse Core Ops, SparseCore 0:
  12.2 63.4 all-gather.1
  99.3 6.6 reduce-scatter.1
Sparse Core Ops, SparseCore 1:
  17.5 132.5 all-reduce.1
where the time goes:
time: 161 us
  waiting for transfers between devices  111 us (69%)
  between operations  15.6 us (10%)
  local copies, waits for them, and re-layouts  13.7 us (9%)
  other arithmetic  12.8 us (8%)
  matrix products  7.62 us (5%)
    all_gather x1, waiting for transfers between devices, body(): lax.all_gather(back_agg, 'graph', axis=0, tiled=True)  60 us
    psum x1, waiting for transfers between devices, body(): weight_grad = lax.psum(partial_weight, ('graph', 'rep'))  51 us
    scatter-add x2, other arithmetic, tile_products(): running.at[local_col[:, slot_index]].add(product * alive[:, None, None])  5.67 us
    gather x2, local copies, waits for them, and re-layouts, tile_products(): chosen = blocks[part_index, local_row[:, slot_index]]  5.41 us
    dot_general x2, matrix products, tile_products(): jnp.einsum('kab,kac->kbc', local_tiles[:, slot_index], chosen, preferred_...  4.91 us
    mul x2, local copies, waits for them, and re-layouts, tile_products(): product * alive[:, None, None]  4.82 us
  transfers between devices with their start and end apart: 3, of which 2 were waited for; matrix products, arithmetic and copies ran while one was open for 19% of the time, Pallas kernels for 0%

commit v1 on v0

--- a/solution.py
+++ b/solution.py
@@ -53,7 +53,7 @@
     input_grad = lax.psum_scatter(
         jnp.take(partial_grad, local_perm, axis=0), "rep", scatter_dimension=0, tiled=True
     ).astype(jnp.bfloat16)
-    weight_grad = lax.psum(partial_weight, ("graph", "rep"))
+    weight_grad = jnp.sum(lax.all_gather(partial_weight, ("graph", "rep")), axis=0)
     return (input_grad, weight_grad, relu_grad)
 
 

time: 161 us -> 204 us (1.27)
  waiting for transfers between devices: 111 us -> 149 us
  local copies, waits for them, and re-layouts: 13.7 us -> 20.8 us
    all_gather x0 -> x1, waiting for transfers between devices: none -> 78.9 us  [body(): lax.all_gather(partial_weight, ('graph', 'rep'))]
    psum x1 -> x0, waiting for transfers between devices: 51 us -> none  [body(): weight_grad = lax.psum(partial_weight, ('graph', 'rep'))]
    unnamed x8 -> x17, local copies, waits for them, and re-layouts: 1.91 us -> 9.01 us
    reduce_scatter x1, waiting for transfers between devices: 0.01 us -> 5.73 us  [body(): lax.psum_scatter(jnp.take(partial_grad, local_perm, axis=0), 'rep', scatt...]
    all_gather x1, waiting for transfers between devices: 60 us -> 64.2 us  [body(): lax.all_gather(back_agg, 'graph', axis=0, tiled=True)]
  transfers between devices with their start and end apart: 3 -> 3, of which waited for: 2 -> 3; matrix products, arithmetic and copies ran while one was open for 19% -> 2% of each run, Pallas kernels for 0% -> 0%
where the time goes in v1:
time: 204 us; the launch traced here: 203 us
  waiting for transfers between devices  149 us (73%)
  local copies, waits for them, and re-layouts  20.8 us (10%)
  between operations  15.7 us (8%)
  other arithmetic  11.2 us (5%)
  matrix products  6.7 us (3%)
    all_gather x1, waiting for transfers between devices, body(): lax.all_gather(partial_weight, ('graph', 'rep'))  78.9 us
    all_gather x1, waiting for transfers between devices, body(): lax.all_gather(back_agg, 'graph', axis=0, tiled=True)  64.2 us
    unnamed x17, local copies, waits for them, and re-layouts  9.01 us
    reduce_scatter x1, waiting for transfers between devices, body(): lax.psum_scatter(jnp.take(partial_grad, local_perm, axis=0), 'rep', scatt...  5.73 us
    scatter-add x2, other arithmetic, tile_products(): running.at[local_col[:, slot_index]].add(product * alive[:, None, None])  5.66 us
    gather x2, local copies, waits for them, and re-layouts, tile_products(): chosen = blocks[part_index, local_row[:, slot_index]]  5.4 us
    dot_general x2, matrix products, tile_products(): jnp.einsum('kab,kac->kbc', local_tiles[:, slot_index], chosen, preferred_...  4.89 us
    mul x2, local copies, waits for them, and re-layouts, tile_products(): product * alive[:, None, None]  4.81 us
  transfers between devices with their start and end apart: 3, of which 3 were waited for; matrix products, arithmetic and copies ran while one was open for 2% of the time, Pallas kernels for 0%

profile of v1, /device:TPU:0, one launch (start us, length us, event | category | flops | bytes accessed | tf_op | source)
XLA Modules:
  0.0 203.5 jit_solution(6314049127749029822)
XLA Ops:
  8.0 0.0 copy-start
  8.0 0.0 copy-start.3
  8.0 0.0 copy-start.6
  8.1 0.0 all-gather.4.cloned.1.call-start
  8.1 1.0 compare_select_fusion
  9.1 0.0 copy-start.1
  9.1 0.9 convolution_convert_fusion
  10.0 0.0 all-gather.4.cloned.1.call-update
  10.0 0.0 reduce-scatter.2.cloned.1.call-start
  10.1 1.3 copy.30
  11.5 64.2 %all-gather.4.cloned.1.call-done = bf16[4096,256]{1,0:T(8,128)(2,1)} async-done(((bf16[256,256]{1,0:T(8,128)(2,1)}), bf16[4096,256]{1,0:T(8,128)(2,1)}) %all-gather.4.cloned.1.call-update) | async-done | bytes 2097168 | tf_op jit(solution)/shard_map/all_gather | solution.py:45
  75.7 2.2 %gather_fusion = bf16[16,128,256]{2,1,0:T(8,128)(2,1)S(1)} fusion(bf16[16,2,128,256]{3,2,1,0:T(8,128)(2,1)} %bitcast.50, s32[16]{0:T(128)S(1)} %get-tuple-element.7), kind=kCustom, calls=%fused_computation | custom fusion | bytes 2097280 | tf_op jit(solution)/shard_map/gather | solution.py:14
  77.9 1.8 multiply_bitcast_fusion.1
  79.7 1.9 copy.22
  81.6 3.2 %gather_fusion.1 = bf16[16,128,256]{2,1,0:T(8,128)(2,1)} fusion(bf16[16,2,128,256]{3,2,1,0:T(8,128)(2,1)} %bitcast.51, s32[16]{0:T(128)S(1)} %get-tuple-element.6), kind=kCustom, calls=%fused_computation.1 | custom fusion | bytes 2097280 | tf_op jit(solution)/shard_map/gather | solution.py:14
  84.8 3.1 %multiply_bitcast_fusion = f32[16,128,256]{1,2,0:T(8,128)} fusion(bf16[16,128,256]{2,1,0:T(8,128)(2,1)} %gather_fusion.1, f32[16]{0:T(128)S(1)} %get-tuple-element.10, bf16[16,2,128,128]{3,2,0,1:T(8,128)(2,1)S(1)} %bitcast.49), kind=kOutput, calls=%fused_computation.6 | convolution fusion | flops 134742016 | bytes 3670528 | tf_op jit(solution)/shard_map/kab,kac->kbc/dot_general | solution.py:15
  87.9 2.9 %copy.24 = f32[16,128,256]{2,1,0:T(8,128)} copy(f32[16,128,256]{1,2,0:T(8,128)} %multiply_bitcast_fusion) | data formatting | bytes 4194304 | tf_op jit(solution)/shard_map/mul | solution.py:19
  90.8 2.2 %scatter_fusion = f32[4,128,256]{2,1,0:T(8,128)S(1)} fusion(f32[4,128,256]{2,1,0:T(8,128)S(1)} %broadcast_in_dim.10, s32[16]{0:T(128)S(1)} %get-tuple-element.9, f32[16,128,256]{2,1,0:T(8,128)S(1)} %copy.22), kind=kCustom, calls=%fused_computation.3 | custom fusion | flops 524288 | bytes 6291520 | tf_op jit(solution)/shard_map/scatter-add | solution.py:19
  93.0 3.5 %scatter_fusion.1 = f32[4,128,256]{2,1,0:T(8,128)S(1)} fusion(f32[4,128,256]{2,1,0:T(8,128)S(1)} %scatter_fusion, s32[16]{0:T(128)S(1)} %get-tuple-element.8, f32[16,128,256]{2,1,0:T(8,128)} %copy.24), kind=kCustom, calls=%fused_computation.4 | custom fusion | flops 524288 | bytes 6291520 | tf_op jit(solution)/shard_map/scatter-add | solution.py:19
  96.5 0.0 copy-start.2
  96.5 1.6 gather_fusion.2
  98.1 1.0 broadcast_select_fusion
  99.1 0.0 reduce-scatter.2.cloned.1.call-update
  99.1 0.0 all-gather.6.cloned.1.call-start
  99.2 0.9 convolution_bitcast_fusion
  100.1 0.0 all-gather.6.cloned.1.call-update
  100.1 5.7 %reduce-scatter.2.cloned.1.call-done = f32[256,256]{1,0:T(8,128)} async-done(((f32[512,256]{1,0:T(8,128)}), f32[256,256]{1,0:T(8,128)}) %reduce-scatter.2.cloned.1.call-update) | async-done | bytes 262160 | tf_op jit(solution)/shard_map/reduce_scatter | solution.py:53
  105.9 1.6 convert_element_type.31
  107.5 78.9 %all-gather.6.cloned.1.call-done = f32[8192,256]{0,1:T(8,128)} async-done(((f32[256,256]{0,1:T(8,128)}), f32[8192,256]{0,1:T(8,128)}) %all-gather.6.cloned.1.call-update) | async-done | bytes 8388624 | tf_op jit(solution)/shard_map/all_gather | solution.py:56
  186.4 6.8 %copy.28 = f32[32,8,32,256]{3,2,1,0:T(8,128)S(1)} copy(f32[32,8,32,256]{3,1,2,0:T(8,128)} %bitcast.47) | data formatting | bytes 16777216
  193.3 1.9 bitcast_reduce_fusion
  195.2 0.8 copy.25
  (16 shorter events, 0.1 us)
Async XLA Ops:
  8.0 1.1 copy-start
  8.0 3.4 %copy-start.3 = (s32[1,512]{1,0:T(1,128)S(1)}, s32[1,512]{1,0:T(1,128)}, u32[]{:S(2)}) copy-start(s32[1,512]{1,0:T(1,128)} %param.17) | copy-start | bytes 6148
  8.0 3.4 %copy-start.6 = (s32[1,1,16]{2,1,0:T(1,128)S(1)}, s32[1,1,16]{2,1,0:T(1,128)}, u32[]{:S(2)}) copy-start(s32[1,1,16]{2,1,0:T(1,128)} %param.16) | copy-start | bytes 196
  8.0 3.4 %copy-start.4 = (s32[1,1,16,2]{2,3,1,0:T(2,128)S(1)}, s32[1,1,16,2]{2,3,1,0:T(2,128)}, u32[]{:S(2)}) copy-start(s32[1,1,16,2]{2,3,1,0:T(2,128)} %param.14) | copy-start | bytes 388
  8.0 3.4 %copy-start.5 = (s32[1,1,16,2]{2,3,1,0:T(2,128)S(1)}, s32[1,1,16,2]{2,3,1,0:T(2,128)}, u32[]{:S(2)}) copy-start(s32[1,1,16,2]{2,3,1,0:T(2,128)} %param.15) | copy-start | bytes 388
  8.1 67.6 %all-gather.4.cloned.1.call-start = ((), (), s32[]{:S(2)}) async-start(), calls=%async_computation.1 | async-start | bytes 2228224 | tf_op jit(solution)/shard_map/all_gather | solution.py:45
  9.1 90.0 %copy-start.1 = (bf16[256,256]{1,0:T(8,128)(2,1)}, bf16[256,256]{1,0:T(8,128)(2,1)S(1)}, u32[]{:S(2)}) copy-start(bf16[256,256]{1,0:T(8,128)(2,1)S(1)} %compare_select_fusion) | copy-start | bytes 393220
  10.0 95.8 %reduce-scatter.2.cloned.1.call-start = ((), (), s32[]{:S(2)}) async-start(), calls=%async_computation.2 | async-start | bytes 786432 | tf_op jit(solution)/shard_map/reduce_scatter | solution.py:53
  96.5 2.7 %copy-start.2 = (bf16[256,256]{1,0:T(8,128)(2,1)S(1)}, bf16[256,256]{1,0:T(8,128)(2,1)}, u32[]{:S(2)}) copy-start(bf16[256,256]{1,0:T(8,128)(2,1)} %param.11) | copy-start | bytes 393220
  99.1 87.3 %all-gather.6.cloned.1.call-start = ((), (), s32[]{:S(2)}) async-start(), calls=%async_computation.3 | async-start | bytes 8650752 | tf_op jit(solution)/shard_map/all_gather | solution.py:56
Sparse Core Ops, SparseCore 0:
  12.2 63.3 all-gather.3
  99.2 6.5 reduce-scatter.1
Sparse Core Ops, SparseCore 1:
  103.5 82.9 all-gather.5
